TPU v7x, 32 devices: a whole 2x2x4 slice. The times are simulated.
32 devices in a mesh: dp: 8 (over y, x, core), head: 4 (over z).
Axes of the slice: x: 2, y: 2, z: 4, core: 2. Of those that a mesh axis runs over, the one named last changes fastest.
Arguments:
- queries: bfloat16 [3072, 512], P('dp', 'head'), may hold values from -8 to 8
- keys: bfloat16 [3072, 128], P('dp'), may hold values from -5 to 5
- values: bfloat16 [3072, 128], P('dp'), may hold values from -6 to 6
- block_of_slot: int32 [16], replicated, may hold values from 0 to 15, as said below
- doc_lengths: int32 [4], replicated, may hold values from 1 to 1536, 3072 in all
- out_weight: bfloat16 [512, 2048], P('head'), may hold values from -0.5 to 0.5
Outputs:
- mixed: bfloat16 [3072, 2048], P(('dp', 'head'))
Inputs may be any that keep to these rules, and one draw needn't show every extreme that they name: `block_of_slot`: a permutation of 0 .. 15; entries 2 i and 2 i + 1 are the two slots of index i of dp, and they add to 15.
All inputs are finite; a program needn't handle non-finite values.
Results may differ from a plain program's by a relative error of at most 0.02.
Values may be sent and summed in bfloat16 or wider, within the bound.
A program may use at most 64 MiB of HBM per device.

v0:
```python
import math

import jax
import jax.numpy as jnp
from jax import lax
from jax.sharding import PartitionSpec as P


def slot_positions(first_row, row_count, table, half_rows):
    row_index = first_row + jnp.arange(row_count, dtype=jnp.int32)
    slot_index = row_index // half_rows
    all_slots = jnp.arange(table.shape[0], dtype=jnp.int32)
    block_id = jnp.sum(
        jnp.where(slot_index[:, None] == all_slots[None, :], table[None, :], 0), axis=1
    )
    return block_id * half_rows + row_index % half_rows


def document_ids(positions, bounds):
    return jnp.sum((positions[:, None] >= bounds[None, :]).astype(jnp.int32), axis=1)


def per_device(queries, keys, values, block_of_slot, doc_lengths, out_weight):
    tok_rows = queries.shape[0]
    head_size = queries.shape[1]
    half_rows = tok_rows // 2
    head_total = lax.axis_size("head")
    group_size = min(8, head_total)
    kv_start = lax.axis_index("head") // group_size * head_size
    own_keys = lax.dynamic_slice_in_dim(keys, kv_start, head_size, 1)
    own_values = lax.dynamic_slice_in_dim(values, kv_start, head_size, 1)
    bounds = jnp.cumsum(doc_lengths)[:-1]
    query_pos = slot_positions(lax.axis_index("dp") * tok_rows, tok_rows, block_of_slot, half_rows)
    query_doc = document_ids(query_pos, bounds)
    score_scale = 1.0 / math.sqrt(head_size)

    def attend(totals, key_block, value_block, allowed):
        run_max, run_sum, run_acc = totals
        scores = (
            jnp.einsum("qd,kd->qk", queries, key_block, preferred_element_type=jnp.float32)
            * score_scale
        )
        masked = jnp.where(allowed, scores, -1e30)
        new_max = jnp.maximum(run_max, jnp.max(masked, axis=1))
        weights = jnp.where(allowed, jnp.exp(masked - new_max[:, None]), 0.0)
        factor = jnp.exp(run_max - new_max)
        new_sum = run_sum * factor + jnp.sum(weights, axis=1)
        new_acc = run_acc * factor[:, None] + jnp.dot(
            weights.astype(jnp.bfloat16), value_block, preferred_element_type=jnp.float32
        )
        return (new_max, new_sum, new_acc)

    initial = (
        jnp.full((tok_rows,), -1e30, jnp.float32),
        jnp.zeros((tok_rows,), jnp.float32),
        jnp.zeros((tok_rows, head_size), jnp.float32),
    )
    totals = initial
    key_piece = lax.all_gather(own_keys, "dp", axis=0, tiled=True)
    value_piece = lax.all_gather(own_values, "dp", axis=0, tiled=True)
    shard_count = key_piece.shape[0] // tok_rows
    per_step = max(
        [1]
        + [
            option_width
            for option_width in range(1, shard_count + 1)
            if shard_count % option_width == 0 and option_width * tok_rows <= 1536
        ]
    )
    step_rows = per_step * tok_rows
    step_count = shard_count // per_step
    key_blocks = key_piece.reshape(step_count, step_rows, head_size)
    value_blocks = value_piece.reshape(step_count, step_rows, head_size)
    step_starts = step_rows * jnp.arange(step_count, dtype=jnp.int32)

    def advance(running, inputs):
        key_block, value_block, block_start = inputs
        key_pos = slot_positions(block_start, step_rows, block_of_slot, half_rows)
        key_doc = document_ids(key_pos, bounds)
        allowed = (query_doc[:, None] == key_doc[None, :]) & (
            key_pos[None, :] <= query_pos[:, None]
        )
        running = lax.cond(
            jnp.any(allowed),
            lambda held: attend(held, key_block, value_block, allowed),
            lambda held: held,
            running,
        )
        return (running, None)

    totals, _ = lax.scan(advance, totals, (key_blocks, value_blocks, step_starts))
    run_max, run_sum, run_acc = totals
    attended = (run_acc / run_sum[:, None]).astype(jnp.bfloat16)
    partial_terms = jnp.dot(attended, out_weight, preferred_element_type=jnp.float32)
    mixed = lax.psum_scatter(
        partial_terms.astype(jnp.bfloat16), "head", scatter_dimension=0, tiled=True
    )
    return mixed


def solution(mesh):
    return jax.shard_map(
        per_device,
        mesh=mesh,
        in_specs=(P("dp", "head"), P("dp", None), P("dp", None), P(), P(), P("head", None)),
        out_specs=P(("dp", "head"), None),
        check_vma=False,
    )
```

profile of v0, /device:TPU:0, one launch (start us, length us, event | category | flops | bytes accessed | tf_op | source)
XLA Modules:
  0.0 91.3 jit_solution(7593905972190038194)
XLA Ops:
  6.6 0.8 select_reduce_fusion.1
  7.4 0.8 reduce-window.4
  8.2 12.2 %all_gather.6 = bf16[3072,128]{1,0:T(8,128)(2,1)S(1)} all-gather(bf16[384,128]{1,0:T(8,128)(2,1)} %param.11), channel_id=1, replica_groups=mesh['dp'=8,'head'=4] {'dp'}, dimensions={0}, use_global_device_ids=true | all-gather | bytes 884736 | tf_op jit(solution)/shard_map/all_gather | solution.py:59
  20.4 10.0 %all_gather.7 = bf16[3072,128]{1,0:T(8,128)(2,1)S(1)} all-gather(bf16[384,128]{1,0:T(8,128)(2,1)} %param.12), channel_id=1, replica_groups=mesh['dp'=8,'head'=4] {'dp'}, dimensions={0}, use_global_device_ids=true | all-gather | bytes 884736 | tf_op jit(solution)/shard_map/all_gather | solution.py:60
  30.5 16.3 %while.16 = (s32[]{:T(128)}, f32[384]{0:T(512)S(1)}, f32[384]{0:T(512)S(1)}, f32[384,128]{1,0:T(8,128)S(1)}, s32[384]{0:T(512)S(1)}, /*index=5*/s32[2]{0:T(128)S...) while((s32[]{:T(128)}, f32[384]{0:T(512)S(1)}, ...), condition=%wide.region_11.12_spmd, body=%wide.region_3.11_spmd.sunk | while | flops 309868800 | bytes 10799459 | solution.py:91
  30.6 0.7 dynamic_slice.39
  31.2 0.7 add_select_fusion.5
  31.9 0.7 select_reduce_fusion.3
  32.7 0.7 fusion.37
  33.5 1.6 %fusion.38 = (pred[]{:T(512)}, pred[384,1536]{0,1:T(32,128)(4,1)S(1)}) fusion(s32[384]{0:T(512)S(1)} %get-tuple-element.395, s32[1536]{0:T(1024)S(1)} %fusion.37, s32[1536]{0:T(1024)S(1)} %convert_reduce_fusion.3, s32[384]{0:T(512)S(1)} %get-tuple-element.391), kind=kLoop, calls=%fused_computation.51.clone.1 | loop fusion | flops 2359295 | bytes 605185 | tf_op jit(solution)/shard_map/while/body/eval_jaxpr/reduce_or | solution.py:84
  35.8 2.9 %conditional.2 = ((f32[384]{0:T(512)S(1)}, f32[384]{0:T(512)S(1)}, f32[384,128]{1,0:T(8,128)S(1)})) conditional(s32[]{:T(128)} %convert_element_type.41, (f32[384]{0:T(512)S(1)}, f32[384]{0:T(512)S(1)}, f32[384,128]{1,0:T(8,128)S(1)}) %tuple.46, (bf16[2,1536,128]{2,1,0:T(8,128)(2,1)S(1)}, s32[]{:T(128)}, bf16[384,128]{1,0:T(8,128)(2,1)}, ...), branch_computations={%region_7.7_spmd, %region_8.10_spmd} | conditional | flops 307397376 | bytes 10150952 | solution.py:83
  35.8 1.5 %fusion.32 = (f32[384]{0:T(512)S(1)}, f32[384,1536]{0,1:T(8,128)S(1)}) fusion(pred[384,1536]{0,1:T(32,128)(4,1)S(1)} %get-tuple-element.215, bf16[384,128]{1,0:T(8,128)(2,1)} %get-tuple-element.218, bf16[2,1536,128]{2,1,0:T(8,128)(2,1)S(1)} %get-tuple-element.216, s32[]{:T(128)} %get-tuple-element.217), kind=kOutput, calls=%fused_computation.52 | convolution fusion | flops 152764032 | bytes 3442180 | tf_op jit(solution)/shard_map/while/body/eval_jaxpr/cond/branch_1_fun/qd,kd->qk/dot_general | solution.py:40
  37.9 0.7 fusion.8
  38.7 0.7 dynamic_slice.39
  39.4 0.7 add_select_fusion.5
  40.1 0.7 select_reduce_fusion.3
  40.9 0.7 fusion.37
  41.7 1.6 %fusion.38 = (pred[]{:T(512)}, pred[384,1536]{0,1:T(32,128)(4,1)S(1)}) fusion(s32[384]{0:T(512)S(1)} %get-tuple-element.395, s32[1536]{0:T(1024)S(1)} %fusion.37, s32[1536]{0:T(1024)S(1)} %convert_reduce_fusion.3, s32[384]{0:T(512)S(1)} %get-tuple-element.391), kind=kLoop, calls=%fused_computation.51.clone.1 | loop fusion | flops 2359295 | bytes 605185 | tf_op jit(solution)/shard_map/while/body/eval_jaxpr/reduce_or | solution.py:84
  44.0 2.9 %conditional.2 = ((f32[384]{0:T(512)S(1)}, f32[384]{0:T(512)S(1)}, f32[384,128]{1,0:T(8,128)S(1)})) conditional(s32[]{:T(128)} %convert_element_type.41, (f32[384]{0:T(512)S(1)}, f32[384]{0:T(512)S(1)}, f32[384,128]{1,0:T(8,128)S(1)}) %tuple.46, (bf16[2,1536,128]{2,1,0:T(8,128)(2,1)S(1)}, s32[]{:T(128)}, bf16[384,128]{1,0:T(8,128)(2,1)}, ...), branch_computations={%region_7.7_spmd, %region_8.10_spmd} | conditional | flops 307397376 | bytes 10150952 | solution.py:83
  44.0 1.5 %fusion.32 = (f32[384]{0:T(512)S(1)}, f32[384,1536]{0,1:T(8,128)S(1)}) fusion(pred[384,1536]{0,1:T(32,128)(4,1)S(1)} %get-tuple-element.215, bf16[384,128]{1,0:T(8,128)(2,1)} %get-tuple-element.218, bf16[2,1536,128]{2,1,0:T(8,128)(2,1)S(1)} %get-tuple-element.216, s32[]{:T(128)} %get-tuple-element.217), kind=kOutput, calls=%fused_computation.52 | convolution fusion | flops 152764032 | bytes 3442180 | tf_op jit(solution)/shard_map/while/body/eval_jaxpr/cond/branch_1_fun/qd,kd->qk/dot_general | solution.py:40
  45.5 0.6 fusion.3
  46.1 0.7 fusion.8
  46.9 1.8 %convolution_convert_fusion = bf16[384,2048]{1,0:T(8,128)(2,1)} fusion(bf16[128,2048]{1,0:T(8,128)(2,1)S(1)} %copy-done, f32[384,128]{1,0:T(8,128)S(1)} %get-tuple-element.240, f32[384]{0:T(512)S(1)} %get-tuple-element.241), kind=kOutput, calls=%fused_computation.33 | convolution fusion | flops 202211328 | bytes 2295296 | tf_op jit(solution)/shard_map/dot_general | solution.py:94
  48.7 35.8 %reduce-scatter.2.cloned.1.call-done = bf16[96,2048]{1,0:T(8,128)(2,1)} async-done(((bf16[384,2048]{1,0:T(8,128)(2,1)}), bf16[96,2048]{1,0:T(8,128)(2,1)}) %reduce-scatter.2.cloned.1.call-update) | async-done | bytes 393232 | tf_op jit(solution)/shard_map/reduce_scatter | solution.py:95
  (21 shorter events, 1.0 us)
Async XLA Ops:
  6.5 40.4 %copy-start = (bf16[128,2048]{1,0:T(8,128)(2,1)S(1)}, bf16[128,2048]{1,0:T(8,128)(2,1)}, u32[]{:S(2)}) copy-start(bf16[128,2048]{1,0:T(8,128)(2,1)} %param.15) | copy-start | bytes 1572868
  6.5 77.9 %reduce-scatter.2.cloned.1.call-start = ((), (), s32[]{:S(2)}) async-start(), calls=%async_computation.1 | async-start | bytes 1966080 | tf_op jit(solution)/shard_map/reduce_scatter | solution.py:95
Sparse Core Ops, SparseCore 0:
  48.8 35.5 reduce-scatter.1
where the time goes:
time: 91.7 us; the launch traced here: 91.3 us
  waiting for transfers between devices  35.8 us (39%)
  blocking collectives  22.2 us (24%)
  between operations  13.4 us (15%)
  other arithmetic  10.8 us (12%)
  matrix products  6.2 us (7%)
  loops' own time  1.53 us (2%)
  local copies, waits for them, and re-layouts  1.37 us (1%)
    reduce_scatter x1, waiting for transfers between devices, per_device(): lax.psum_scatter(partial_terms.astype(jnp.bfloat16), 'head', scatter_dime...  35.8 us
    all_gather x1, blocking collectives, per_device(): key_piece = lax.all_gather(own_keys, 'dp', axis=0, tiled=True)  12.2 us
    all_gather x1, blocking collectives, per_device(): value_piece = lax.all_gather(own_values, 'dp', axis=0, tiled=True)  10 us
    reduce_or x2, other arithmetic, advance(): jnp.any(allowed)  3.29 us
    dot_general x2, matrix products, attend(): jnp.einsum('qd,kd->qk', queries, key_block, preferred_element_type=jnp.fl...  2.93 us
    reduce_sum x3, other arithmetic, slot_positions(): jnp.sum(jnp.where(slot_index[:, None] == all_slots[None, :], table[None,...  2.29 us
  transfers between devices with their start and end apart: 1, of which 1 were waited for; matrix products, arithmetic and copies ran while one was open for 0% of the time, Pallas kernels for 0%

commit v1 on v0

--- a/solution.py
+++ b/solution.py
@@ -1,9 +1,15 @@
+import functools
 import math
 
 import jax
 import jax.numpy as jnp
 from jax import lax
+from jax.experimental import pallas as pl
+from jax.experimental.pallas import tpu as pltpu
 from jax.sharding import PartitionSpec as P
+
+MESH = pl.DeviceIdType.MESH
+NEG = -1e30
 
 
 def slot_positions(first_row, row_count, table, half_rows):
@@ -20,7 +26,7 @@
     return jnp.sum((positions[:, None] >= bounds[None, :]).astype(jnp.int32), axis=1)
 
 
-def per_device(queries, keys, values, block_of_slot, doc_lengths, out_weight):
+def general(queries, keys, values, block_of_slot, doc_lengths, out_weight):
     tok_rows = queries.shape[0]
     head_size = queries.shape[1]
     half_rows = tok_rows // 2
@@ -29,7 +35,9 @@
     kv_start = lax.axis_index("head") // group_size * head_size
     own_keys = lax.dynamic_slice_in_dim(keys, kv_start, head_size, 1)
     own_values = lax.dynamic_slice_in_dim(values, kv_start, head_size, 1)
-    bounds = jnp.cumsum(doc_lengths)[:-1]
+    count = doc_lengths.shape[0]
+    before = jnp.arange(count)[None, :] <= jnp.arange(count - 1)[:, None]
+    bounds = jnp.sum(jnp.where(before, doc_lengths[None, :], 0), axis=1)
     query_pos = slot_positions(lax.axis_index("dp") * tok_rows, tok_rows, block_of_slot, half_rows)
     query_doc = document_ids(query_pos, bounds)
     score_scale = 1.0 / math.sqrt(head_size)
@@ -40,7 +48,7 @@
             jnp.einsum("qd,kd->qk", queries, key_block, preferred_element_type=jnp.float32)
             * score_scale
         )
-        masked = jnp.where(allowed, scores, -1e30)
+        masked = jnp.where(allowed, scores, NEG)
         new_max = jnp.maximum(run_max, jnp.max(masked, axis=1))
         weights = jnp.where(allowed, jnp.exp(masked - new_max[:, None]), 0.0)
         factor = jnp.exp(run_max - new_max)
@@ -50,12 +58,11 @@
         )
         return (new_max, new_sum, new_acc)
 
-    initial = (
-        jnp.full((tok_rows,), -1e30, jnp.float32),
+    totals = (
+        jnp.full((tok_rows,), NEG, jnp.float32),
         jnp.zeros((tok_rows,), jnp.float32),
         jnp.zeros((tok_rows, head_size), jnp.float32),
     )
-    totals = initial
     key_piece = lax.all_gather(own_keys, "dp", axis=0, tiled=True)
     value_piece = lax.all_gather(own_values, "dp", axis=0, tiled=True)
     shard_count = key_piece.shape[0] // tok_rows
@@ -92,13 +99,284 @@
     run_max, run_sum, run_acc = totals
     attended = (run_acc / run_sum[:, None]).astype(jnp.bfloat16)
     partial_terms = jnp.dot(attended, out_weight, preferred_element_type=jnp.float32)
-    mixed = lax.psum_scatter(
+    return lax.psum_scatter(
         partial_terms.astype(jnp.bfloat16), "head", scatter_dimension=0, tiled=True
     )
-    return mixed
+
+
+def flip(index, bit):
+    return index + bit - 2 * bit * lax.rem(lax.div(index, bit), 2)
+
+
+def flipped(index, mask):
+    bit = 1
+    while bit <= mask:
+        if mask & bit:
+            index = flip(index, bit)
+        bit *= 2
+    return index
+
+
+CORE, ALONG_X, ALONG_Y = 1, 2, 4
+DIAG = ALONG_X + ALONG_Y
+
+
+def fused_kernel(
+    dp_total, head_total, table, lengths, q_in, k_in, v_in, w_in, out_ref,
+    q_buf, k_buf, v_buf, w_buf, att_buf,
+    local_sem, q_send, q_recv, k_send, k_recv, v_send, v_recv, z_send, z_recv, w_send, w_recv,
+):
+    me, head = lax.axis_index("dp"), lax.axis_index("head")
+    rows, head_size = q_buf.shape[1:]
+    tok_rows = k_buf.shape[1]
+    half_rows = tok_rows // 2
+    width = w_buf.shape[-1]
+    near = {mask: flipped(me, mask) for mask in range(dp_total)}
+    heads = {mask: flipped(head, mask) for mask in range(head_total)}
+
+    barrier = pltpu.get_barrier_semaphore()
+    for mask in (CORE, ALONG_X, ALONG_Y):
+        pl.semaphore_signal(barrier, inc=1, device_id=(near[mask], head), device_id_type=MESH)
+    for mask in range(1, head_total):
+        pl.semaphore_signal(barrier, inc=1, device_id=(me, heads[mask]), device_id_type=MESH)
+
+    def own_rows(of_head):
+        return q_in.at[pl.ds(pl.multiple_of(of_head * rows, 16), rows)]
+
+    locals_ = [
+        pltpu.make_async_copy(k_in, k_buf.at[0], local_sem.at[0]),
+        pltpu.make_async_copy(v_in, v_buf.at[0], local_sem.at[1]),
+        pltpu.make_async_copy(own_rows(head), q_buf.at[0], local_sem.at[2]),
+        pltpu.make_async_copy(w_in, w_buf.at[0], local_sem.at[3]),
+    ]
+    for copy in locals_:
+        copy.start()
+    pl.semaphore_wait(barrier, 3 + head_total - 1)
+
+    sent = []
+
+    def send(src, dst, send_sem, recv_sem, to):
+        copy = pltpu.make_async_remote_copy(
+            src_ref=src, dst_ref=dst, send_sem=send_sem, recv_sem=recv_sem,
+            device_id=to, device_id_type=MESH,
+        )
+        copy.start()
+        sent.append(copy)
+
+    def arrived(dst, recv_sem):
+        pltpu.make_async_remote_copy(
+            src_ref=dst, dst_ref=dst, send_sem=recv_sem, recv_sem=recv_sem,
+            device_id=(near[CORE], head), device_id_type=MESH,
+        ).wait_recv()
+
+    def pass_on(buf, send_sems, recv_sems, slot, mask, src=None):
+        landing = slot ^ mask
+        number = landing * 3 + (CORE, ALONG_X, ALONG_Y).index(mask)
+        send(
+            buf.at[slot] if src is None else src, buf.at[landing],
+            send_sems.at[number], recv_sems.at[landing], (near[mask], head),
+        )
+
+    def k_pass(slot, mask, src=None):
+        pass_on(k_buf, k_send, k_recv, slot, mask, src)
+
+    def v_pass(slot, mask, src=None):
+        pass_on(v_buf, v_send, v_recv, slot, mask, src)
+
+    def k_wait(slot):
+        arrived(k_buf.at[slot], k_recv.at[slot])
+
+    def v_wait(slot):
+        arrived(v_buf.at[slot], v_recv.at[slot])
+
+    def w_part(origin, half):
+        columns = pl.ds(0, width) if half is None else pl.ds(half * (width // 2), width // 2)
+        return w_buf.at[pl.ds(1, head_total - 1), near[origin], :, columns]
+
+    def w_number(origin, half):
+        return origin if origin & DIAG != DIAG else dp_total + 2 * (origin & 1) + half
+
+    def w_pass(slot, mask, half=None):
+        landing = slot ^ mask
+        number = w_number(landing, half)
+        send(
+            w_part(slot, half), w_part(slot, half),
+            w_send.at[number * 3 + (CORE, ALONG_X, ALONG_Y).index(mask)], w_recv.at[number],
+            (near[mask], head),
+        )
+
+    def w_wait(slot, half=None):
+        arrived(w_part(slot, half), w_recv.at[w_number(slot, half)])
+
+    for mask in range(1, head_total):
+        send(own_rows(heads[mask]), q_buf.at[mask], q_send.at[mask], q_recv.at[mask], (me, heads[mask]))
+    k_pass(0, ALONG_X, k_in)
+    v_pass(0, ALONG_Y, v_in)
+    for mask in range(1, head_total):
+        send(w_in.at[me], w_buf.at[mask, me], z_send.at[mask], z_recv.at[mask], (me, heads[mask]))
+    v_pass(0, ALONG_X, v_in)
+    k_pass(0, ALONG_Y, k_in)
+    k_pass(0, CORE, k_in)
+    v_pass(0, CORE, v_in)
+
+    first_slot = me * 2 + lax.div(head * rows, half_rows)
+    first_pos = table[first_slot] * half_rows + lax.rem(head * rows, half_rows)
+    query_pos = first_pos + lax.broadcasted_iota(jnp.int32, (rows, 1), 0)
+    low = jnp.zeros((rows, 1), jnp.int32)
+    bound = jnp.int32(0)
+    for i in range(lengths.shape[0] - 1):
+        bound = bound + lengths[i]
+        low = jnp.where(query_pos >= bound, bound, low)
+    lane = lax.broadcasted_iota(jnp.int32, (1, tok_rows), 1)
+    exponent = math.log2(math.e) / math.sqrt(head_size)
+    total_rows = head_total * rows
+
+    def scores_of(slot):
+        start0 = table[near[slot] * 2] * half_rows
+        start1 = table[near[slot] * 2 + 1] * half_rows - half_rows
+        key_pos = lane + jnp.where(lane < half_rows, start0, start1)
+        allowed = (key_pos <= query_pos) & (key_pos >= low)
+        scores = lax.dot_general(
+            q_buf[...].reshape(total_rows, head_size), k_buf[slot],
+            (((1,), (1,)), ((), ())), preferred_element_type=jnp.float32,
+        ).reshape(head_total, rows, tok_rows)
+        return jnp.where(allowed[None], scores, NEG).reshape(total_rows, tok_rows)
+
+    def fold(totals, slot):
+        masked = scores_of(slot)
+        top = jnp.max(masked, axis=1, keepdims=True)
+        new_max = top if totals is None else jnp.maximum(totals[0], top)
+        weights = jnp.exp2((masked - new_max) * exponent)
+        added = jnp.sum(weights, axis=1, keepdims=True)
+        product = jnp.dot(weights.astype(jnp.bfloat16), v_buf[slot], preferred_element_type=jnp.float32)
+        if totals is None:
+            return new_max, added, product
+        factor = jnp.exp2((totals[0] - new_max) * exponent)
+        return new_max, totals[1] * factor + added, totals[2] * factor + product
+
+    k_wait(ALONG_X)
+    k_pass(ALONG_X, ALONG_Y)
+    k_pass(ALONG_X, CORE)
+    v_wait(ALONG_Y)
+    v_pass(ALONG_Y, ALONG_X)
+    v_pass(ALONG_Y, CORE)
+    for mask in range(1, head_total):
+        arrived(w_buf.at[mask, me], z_recv.at[mask])
+    w_pass(0, ALONG_X)
+    w_pass(0, ALONG_Y)
+    w_pass(0, CORE)
+    v_wait(ALONG_X)
+    v_pass(ALONG_X, CORE)
+    k_wait(ALONG_Y)
+    k_pass(ALONG_Y, CORE)
+    for copy in locals_:
+        copy.wait()
+    for mask in range(1, head_total):
+        arrived(q_buf.at[mask], q_recv.at[mask])
+    totals = fold(None, 0)
+    k_wait(DIAG)
+    k_pass(DIAG, CORE)
+    v_wait(DIAG)
+    v_pass(DIAG, CORE)
+    totals = fold(totals, ALONG_X)
+    w_wait(ALONG_X)
+    w_pass(ALONG_X, ALONG_Y, 0)
+    w_pass(ALONG_X, CORE)
+    w_wait(ALONG_Y)
+    w_pass(ALONG_Y, ALONG_X, 1)
+    w_pass(ALONG_Y, CORE)
+    totals = fold(totals, ALONG_Y)
+    for slot in (CORE, CORE + ALONG_X, CORE + ALONG_Y):
+        k_wait(slot)
+        v_wait(slot)
+        totals = fold(totals, slot)
+    for half in (0, 1):
+        w_wait(DIAG, half)
+        w_pass(DIAG, CORE, half)
+    totals = fold(totals, DIAG)
+    k_wait(CORE + DIAG)
+    v_wait(CORE + DIAG)
+    _, run_sum, run_acc = fold(totals, CORE + DIAG)
+    attended = (run_acc / run_sum).astype(jnp.bfloat16)
+    for mask in range(head_total):
+        att_buf[:, mask * head_size : (mask + 1) * head_size] = attended[mask * rows : (mask + 1) * rows]
+    w_wait(CORE)
+    w_wait(CORE + ALONG_X)
+    w_wait(CORE + ALONG_Y)
+    w_wait(CORE + DIAG, 0)
+    w_wait(CORE + DIAG, 1)
+    step = min(width, 512)
+    for start in range(0, width, step):
+        block = w_buf[:, :, :, start : start + step].reshape(head_total * head_size, step)
+        out_ref[:, start : start + step] = jnp.dot(
+            att_buf[...], block, preferred_element_type=jnp.float32
+        ).astype(out_ref.dtype)
+    for copy in sent:
+        copy.wait_send()
+
+
+def fused(dp_total, head_total, queries, keys, values, block_of_slot, doc_lengths, out_weight):
+    tok_rows, head_size = queries.shape
+    rows = tok_rows // head_total
+    depth, width = out_weight.shape
+    any_, smem, vmem = (pl.BlockSpec(memory_space=m) for m in (pl.ANY, pltpu.SMEM, pltpu.VMEM))
+    dma = pltpu.SemaphoreType.DMA
+    piece = depth // dp_total
+    return pl.pallas_call(
+        functools.partial(fused_kernel, dp_total, head_total),
+        out_shape=jax.ShapeDtypeStruct((rows, width), jnp.bfloat16),
+        in_specs=[smem, smem, any_, any_, any_, any_],
+        out_specs=vmem,
+        scratch_shapes=[
+            pltpu.VMEM((head_total, rows, head_size), jnp.bfloat16),
+            pltpu.VMEM((dp_total, tok_rows, head_size), jnp.bfloat16),
+            pltpu.VMEM((dp_total, tok_rows, head_size), jnp.bfloat16),
+            pltpu.VMEM((head_total, dp_total, piece, width), jnp.bfloat16),
+            pltpu.VMEM((rows, head_total * head_size), jnp.bfloat16),
+            dma((4,)),
+            dma((head_total,)),
+            dma((head_total,)),
+            dma((3 * dp_total,)),
+            dma((dp_total,)),
+            dma((3 * dp_total,)),
+            dma((dp_total,)),
+            dma((head_total,)),
+            dma((head_total,)),
+            dma((3 * (dp_total + 4),)),
+            dma((dp_total + 4,)),
+        ],
+        compiler_params=pltpu.CompilerParams(
+            collective_id=0, has_side_effects=True, vmem_limit_bytes=48 * 2**20
+        ),
+        cost_estimate=pl.CostEstimate(
+            flops=4 * tok_rows * tok_rows * dp_total * head_size + 2 * rows * head_total * depth * width,
+            bytes_accessed=2 * (rows * width + depth * width + 3 * tok_rows * head_size),
+            transcendentals=tok_rows * tok_rows * dp_total,
+        ),
+    )(
+        block_of_slot, doc_lengths, queries, keys, values,
+        out_weight.reshape(dp_total, piece, width),
+    )
 
 
 def solution(mesh):
+    dp_total, head_total = mesh.shape["dp"], mesh.shape["head"]
+
+    def per_device(queries, keys, values, block_of_slot, doc_lengths, out_weight):
+        tok_rows, head_size = queries.shape
+        rows = tok_rows // head_total
+        fits = (
+            dp_total == 2 ** 3
+            and head_total & (head_total - 1) == 0
+            and keys.shape[1] == head_size
+            and rows % 16 == 0
+            and (tok_rows // 2) % rows == 0
+            and out_weight.shape[0] % (16 * dp_total) == 0
+            and out_weight.shape[0] == head_size
+        )
+        run = functools.partial(fused, dp_total, head_total) if fits else general
+        return run(queries, keys, values, block_of_slot, doc_lengths, out_weight)
+
     return jax.shard_map(
         per_device,
         mesh=mesh,

time: 91.7 us -> 31.7 us (0.35)
  the two profiles are of different devices: /device:TPU:0 before, /device:TPU:9 now
where the time goes in v1:
time: 31.7 us; the launch traced here: 31.4 us
  Pallas kernels  26.3 us (83%)
  local copies, waits for them, and re-layouts  5.14 us (16%)
    pallas_call x1, Pallas kernels, fused(): pl.pallas_call(functools.partial(fused_kernel, dp_total, head_total), out...  26.3 us
    unnamed x13, local copies, waits for them, and re-layouts  5.14 us

profile of v1, /device:TPU:9, one launch (start us, length us, event | category | flops | bytes accessed | tf_op | source)
XLA Modules:
  0.0 31.4 jit_solution(8336089969097746243)
XLA Ops:
  0.0 0.0 copy-start.5
  0.0 0.0 copy-start.4
  0.0 0.7 %copy-done.5 = s32[4]{0:T(128)S(1)} copy-done((s32[4]{0:T(128)S(1)}, s32[4]{0:T(128)}, u32[]{:S(2)}) %copy-start.5) | copy-done | bytes 40
  0.7 0.0 copy-done.4
  0.7 0.0 copy-start
  0.7 1.0 %copy-done = bf16[128,2048]{1,0:T(8,128)(2,1)S(1)} copy-done((bf16[128,2048]{1,0:T(8,128)(2,1)S(1)}, bf16[128,2048]{1,0:T(8,128)(2,1)}, u32[]{:S(2)}) %copy-start) | copy-done | bytes 524312
  1.7 0.0 copy-start.1
  1.7 0.9 %copy-done.1 = bf16[384,128]{1,0:T(8,128)(2,1)S(1)} copy-done((bf16[384,128]{1,0:T(8,128)(2,1)S(1)}, bf16[384,128]{1,0:T(8,128)(2,1)}, u32[]{:S(2)}) %copy-start.1) | copy-done | bytes 98328
  2.6 0.0 copy-start.2
  2.6 0.9 %copy-done.2 = bf16[384,128]{1,0:T(8,128)(2,1)S(1)} copy-done((bf16[384,128]{1,0:T(8,128)(2,1)S(1)}, bf16[384,128]{1,0:T(8,128)(2,1)}, u32[]{:S(2)}) %copy-start.2) | copy-done | bytes 98328
  3.5 0.0 copy-start.3
  3.5 0.9 %copy-done.3 = bf16[384,128]{1,0:T(8,128)(2,1)S(1)} copy-done((bf16[384,128]{1,0:T(8,128)(2,1)S(1)}, bf16[384,128]{1,0:T(8,128)(2,1)}, u32[]{:S(2)}) %copy-start.3) | copy-done | bytes 98328
  4.4 26.3 %shard_map.64 = bf16[96,2048]{1,0:T(8,128)(2,1)S(1)} custom-call(s32[16]{0:T(128)S(1)} %copy-done.4, s32[4]{0:T(128)S(1)} %copy-done.5, bf16[384,128]{1,0:T(8,128)(2,1)S(1)} %copy-done.1, bf16[384,128]{1,0:T(8,128)(2,1)S(1)} %copy-done.2, bf16[384,128]{1,0:T(8,128)(2,1)S(1)} %copy-done.3, bf16[8,16,2048]{2,1,0:T(8,128)(2,1)S(1)} %bitcast.1), custom_call_target="tpu_custom_call" | custom-call | flops 805306368 | bytes 1212416 | tf_op jit(solution)/shard_map/pallas_call | solution.py:325
  30.7 0.7 %copy.8 = bf16[96,2048]{1,0:T(8,128)(2,1)} copy(bf16[96,2048]{1,0:T(8,128)(2,1)S(1)} %shard_map.64) | data formatting | bytes 786432
Async XLA Ops:
  0.0 0.7 %copy-start.5 = (s32[4]{0:T(128)S(1)}, s32[4]{0:T(128)}, u32[]{:S(2)}) copy-start(s32[4]{0:T(128)} %lengths.1) | copy-start | bytes 52
  0.0 0.7 %copy-start.4 = (s32[16]{0:T(128)S(1)}, s32[16]{0:T(128)}, u32[]{:S(2)}) copy-start(s32[16]{0:T(128)} %table.1) | copy-start | bytes 196
  0.7 1.0 %copy-start = (bf16[128,2048]{1,0:T(8,128)(2,1)S(1)}, bf16[128,2048]{1,0:T(8,128)(2,1)}, u32[]{:S(2)}) copy-start(bf16[128,2048]{1,0:T(8,128)(2,1)} %param.11) | copy-start | bytes 1572868
  1.7 0.9 %copy-start.1 = (bf16[384,128]{1,0:T(8,128)(2,1)S(1)}, bf16[384,128]{1,0:T(8,128)(2,1)}, u32[]{:S(2)}) copy-start(bf16[384,128]{1,0:T(8,128)(2,1)} %q_in.1) | copy-start | bytes 294916
  2.6 0.9 %copy-start.2 = (bf16[384,128]{1,0:T(8,128)(2,1)S(1)}, bf16[384,128]{1,0:T(8,128)(2,1)}, u32[]{:S(2)}) copy-start(bf16[384,128]{1,0:T(8,128)(2,1)} %k_in.1) | copy-start | bytes 294916
  3.5 0.9 %copy-start.3 = (bf16[384,128]{1,0:T(8,128)(2,1)S(1)}, bf16[384,128]{1,0:T(8,128)(2,1)}, u32[]{:S(2)}) copy-start(bf16[384,128]{1,0:T(8,128)(2,1)} %v_in.1) | copy-start | bytes 294916

commit v2 on v1

--- a/solution.py
+++ b/solution.py
@@ -122,15 +122,16 @@
 
 
 def fused_kernel(
-    dp_total, head_total, table, lengths, q_in, k_in, v_in, w_in, out_ref,
+    dp_total, head_total, shared, table, lengths, q_in, k_in, v_in, w_in, out_ref,
     q_buf, k_buf, v_buf, w_buf, att_buf,
-    local_sem, q_send, q_recv, k_send, k_recv, v_send, v_recv, z_send, z_recv, w_send, w_recv,
+    local_sem, q_send, q_recv, k_send, k_recv, v_send, v_recv, z_send, z_recv, w_send, w_recv, s_send, s_recv,
 ):
     me, head = lax.axis_index("dp"), lax.axis_index("head")
     rows, head_size = q_buf.shape[1:]
     tok_rows = k_buf.shape[1]
     half_rows = tok_rows // 2
-    width = w_buf.shape[-1]
+    depth, width = w_buf.shape[1:]
+    piece = width // dp_total
     near = {mask: flipped(me, mask) for mask in range(dp_total)}
     heads = {mask: flipped(head, mask) for mask in range(head_total)}
 
@@ -189,35 +190,56 @@
     def v_wait(slot):
         arrived(v_buf.at[slot], v_recv.at[slot])
 
-    def w_part(origin, half):
-        columns = pl.ds(0, width) if half is None else pl.ds(half * (width // 2), width // 2)
-        return w_buf.at[pl.ds(1, head_total - 1), near[origin], :, columns]
+    def columns_of(origin):
+        return pl.ds(pl.multiple_of(near[origin] * piece, 128), piece)
+
+    def w_part(foreign, origin, half):
+        span = pl.ds(0, shared) if half is None else pl.ds(half * (shared // 2), shared // 2)
+        return w_buf.at[foreign, span, columns_of(origin)]
 
     def w_number(origin, half):
-        return origin if origin & DIAG != DIAG else dp_total + 2 * (origin & 1) + half
-
-    def w_pass(slot, mask, half=None):
-        landing = slot ^ mask
-        number = w_number(landing, half)
+        return origin if origin & DIAG != DIAG else dp_total + 2 * (origin & 1) + (half or 0)
+
+    def w_pass(foreign, slot, mask, half=None):
+        number = w_number(slot ^ mask, half)
         send(
-            w_part(slot, half), w_part(slot, half),
-            w_send.at[number * 3 + (CORE, ALONG_X, ALONG_Y).index(mask)], w_recv.at[number],
-            (near[mask], head),
-        )
-
-    def w_wait(slot, half=None):
-        arrived(w_part(slot, half), w_recv.at[w_number(slot, half)])
-
-    for mask in range(1, head_total):
-        send(own_rows(heads[mask]), q_buf.at[mask], q_send.at[mask], q_recv.at[mask], (me, heads[mask]))
+            w_part(foreign, slot, half), w_part(foreign, slot, half),
+            w_send.at[foreign, number * 3 + (CORE, ALONG_X, ALONG_Y).index(mask)],
+            w_recv.at[foreign, number], (near[mask], head),
+        )
+
+    def w_wait(foreign, slot, half=None):
+        arrived(w_part(foreign, slot, half), w_recv.at[foreign, w_number(slot, half)])
+
+    def straight(of_core):
+        half_span = (depth - shared) // 2
+        return pl.ds(pl.multiple_of(shared + of_core * half_span, 16), half_span)
+
+    def straight_to_core(foreign):
+        part = w_buf.at[foreign, straight(lax.rem(me, 2))]
+        arrived(part, s_recv.at[0, foreign])
+        send(part, part, s_send.at[1, foreign], s_recv.at[1, foreign], (near[CORE], head))
+
     k_pass(0, ALONG_X, k_in)
     v_pass(0, ALONG_Y, v_in)
     for mask in range(1, head_total):
-        send(w_in.at[me], w_buf.at[mask, me], z_send.at[mask], z_recv.at[mask], (me, heads[mask]))
+        send(
+            w_in.at[pl.ds(0, shared), columns_of(0)], w_part(mask, 0, None),
+            z_send.at[mask], z_recv.at[mask], (me, heads[mask]),
+        )
     v_pass(0, ALONG_X, v_in)
     k_pass(0, ALONG_Y, k_in)
     k_pass(0, CORE, k_in)
     v_pass(0, CORE, v_in)
+    for mask in range(1, head_total):
+        send(own_rows(heads[mask]), q_buf.at[mask], q_send.at[mask], q_recv.at[mask], (me, heads[mask]))
+    if shared < depth:
+        span = straight(lax.rem(me, 2))
+        for mask in range(1, head_total):
+            send(
+                w_in.at[span], w_buf.at[mask, span],
+                s_send.at[0, mask], s_recv.at[0, mask], (me, heads[mask]),
+            )
 
     first_slot = me * 2 + lax.div(head * rows, half_rows)
     first_pos = table[first_slot] * half_rows + lax.rem(head * rows, half_rows)
@@ -254,63 +276,91 @@
         factor = jnp.exp2((totals[0] - new_max) * exponent)
         return new_max, totals[1] * factor + added, totals[2] * factor + product
 
+    foreign_heads = range(1, head_total)
+
+    def w_spread(foreign):
+        arrived(w_part(foreign, 0, None), z_recv.at[foreign])
+        for mask in (ALONG_X, ALONG_Y, CORE):
+            w_pass(foreign, 0, mask)
+
+    def w_second(foreign):
+        w_wait(foreign, ALONG_X)
+        w_pass(foreign, ALONG_X, ALONG_Y, 0)
+        w_pass(foreign, ALONG_X, CORE)
+        w_wait(foreign, ALONG_Y)
+        w_pass(foreign, ALONG_Y, ALONG_X, 1)
+        w_pass(foreign, ALONG_Y, CORE)
+
+    def w_third(foreign):
+        for half in (0, 1):
+            w_wait(foreign, DIAG, half)
+            w_pass(foreign, DIAG, CORE, half)
+
     k_wait(ALONG_X)
     k_pass(ALONG_X, ALONG_Y)
     k_pass(ALONG_X, CORE)
     v_wait(ALONG_Y)
     v_pass(ALONG_Y, ALONG_X)
     v_pass(ALONG_Y, CORE)
-    for mask in range(1, head_total):
-        arrived(w_buf.at[mask, me], z_recv.at[mask])
-    w_pass(0, ALONG_X)
-    w_pass(0, ALONG_Y)
-    w_pass(0, CORE)
+    w_spread(1)
     v_wait(ALONG_X)
     v_pass(ALONG_X, CORE)
     k_wait(ALONG_Y)
     k_pass(ALONG_Y, CORE)
-    for copy in locals_:
-        copy.wait()
-    for mask in range(1, head_total):
-        arrived(q_buf.at[mask], q_recv.at[mask])
-    totals = fold(None, 0)
+    for foreign in foreign_heads[1:]:
+        w_spread(foreign)
     k_wait(DIAG)
     k_pass(DIAG, CORE)
     v_wait(DIAG)
     v_pass(DIAG, CORE)
-    totals = fold(totals, ALONG_X)
-    w_wait(ALONG_X)
-    w_pass(ALONG_X, ALONG_Y, 0)
-    w_pass(ALONG_X, CORE)
-    w_wait(ALONG_Y)
-    w_pass(ALONG_Y, ALONG_X, 1)
-    w_pass(ALONG_Y, CORE)
-    totals = fold(totals, ALONG_Y)
-    for slot in (CORE, CORE + ALONG_X, CORE + ALONG_Y):
-        k_wait(slot)
-        v_wait(slot)
+    for copy in locals_:
+        copy.wait()
+    for mask in foreign_heads:
+        arrived(q_buf.at[mask], q_recv.at[mask])
+    slots = [0, ALONG_X, ALONG_Y, CORE, CORE + ALONG_X, CORE + ALONG_Y, DIAG, CORE + DIAG]
+    totals = None
+    for slot in slots:
+        if slot & CORE:
+            k_wait(slot)
+            v_wait(slot)
         totals = fold(totals, slot)
-    for half in (0, 1):
-        w_wait(DIAG, half)
-        w_pass(DIAG, CORE, half)
-    totals = fold(totals, DIAG)
-    k_wait(CORE + DIAG)
-    v_wait(CORE + DIAG)
-    _, run_sum, run_acc = fold(totals, CORE + DIAG)
+        number = slots.index(slot)
+        if number % 2 and number // 2 < len(foreign_heads):
+            w_second(foreign_heads[number // 2])
+    for foreign in foreign_heads[(len(slots) // 2) :]:
+        w_second(foreign)
+    if shared < depth:
+        for foreign in foreign_heads:
+            straight_to_core(foreign)
+    _, run_sum, run_acc = totals
     attended = (run_acc / run_sum).astype(jnp.bfloat16)
     for mask in range(head_total):
         att_buf[:, mask * head_size : (mask + 1) * head_size] = attended[mask * rows : (mask + 1) * rows]
-    w_wait(CORE)
-    w_wait(CORE + ALONG_X)
-    w_wait(CORE + ALONG_Y)
-    w_wait(CORE + DIAG, 0)
-    w_wait(CORE + DIAG, 1)
-    step = min(width, 512)
-    for start in range(0, width, step):
-        block = w_buf[:, :, :, start : start + step].reshape(head_total * head_size, step)
-        out_ref[:, start : start + step] = jnp.dot(
-            att_buf[...], block, preferred_element_type=jnp.float32
+    if shared < depth:
+        for foreign in foreign_heads:
+            arrived(w_buf.at[foreign, straight(1 - lax.rem(me, 2))], s_recv.at[1, foreign])
+
+    def project(slot):
+        columns = columns_of(slot)
+        out_ref[:, columns] = jnp.dot(
+            att_buf[...], w_buf[:, :, columns].reshape(head_total * depth, piece),
+            preferred_element_type=jnp.float32,
         ).astype(out_ref.dtype)
+
+    project(0)
+    project(ALONG_X)
+    project(ALONG_Y)
+    for foreign in foreign_heads:
+        w_third(foreign)
+    for slot in (CORE, CORE + ALONG_X, CORE + ALONG_Y):
+        for foreign in foreign_heads:
+            w_wait(foreign, slot)
+        project(slot)
+    project(DIAG)
+    for foreign in foreign_heads:
+        w_wait(foreign, CORE + DIAG, 0)
+        w_wait(foreign, CORE + DIAG, 1)
+    project(CORE + DIAG)
     for copy in sent:
         copy.wait_send()
 
@@ -321,9 +371,9 @@
     depth, width = out_weight.shape
     any_, smem, vmem = (pl.BlockSpec(memory_space=m) for m in (pl.ANY, pltpu.SMEM, pltpu.VMEM))
     dma = pltpu.SemaphoreType.DMA
-    piece = depth // dp_total
+    shared = depth * 3 // 4 // 32 * 32
     return pl.pallas_call(
-        functools.partial(fused_kernel, dp_total, head_total),
+        functools.partial(fused_kernel, dp_total, head_total, shared),
         out_shape=jax.ShapeDtypeStruct((rows, width), jnp.bfloat16),
         in_specs=[smem, smem, any_, any_, any_, any_],
         out_specs=vmem,
@@ -331,7 +381,7 @@
             pltpu.VMEM((head_total, rows, head_size), jnp.bfloat16),
             pltpu.VMEM((dp_total, tok_rows, head_size), jnp.bfloat16),
             pltpu.VMEM((dp_total, tok_rows, head_size), jnp.bfloat16),
-            pltpu.VMEM((head_total, dp_total, piece, width), jnp.bfloat16),
+            pltpu.VMEM((head_total, depth, width), jnp.bfloat16),
             pltpu.VMEM((rows, head_total * head_size), jnp.bfloat16),
             dma((4,)),
             dma((head_total,)),
@@ -342,11 +392,13 @@
             dma((dp_total,)),
             dma((head_total,)),
             dma((head_total,)),
-            dma((3 * (dp_total + 4),)),
-            dma((dp_total + 4,)),
+            dma((head_total, 3 * (dp_total + 4))),
+            dma((head_total, dp_total + 4)),
+            dma((2, head_total)),
+            dma((2, head_total)),
         ],
         compiler_params=pltpu.CompilerParams(
-            collective_id=0, has_side_effects=True, vmem_limit_bytes=48 * 2**20
+            collective_id=0, has_side_effects=True, vmem_limit_bytes=60 * 2**20
         ),
         cost_estimate=pl.CostEstimate(
             flops=4 * tok_rows * tok_rows * dp_total * head_size + 2 * rows * head_total * depth * width,
@@ -354,8 +406,7 @@
             transcendentals=tok_rows * tok_rows * dp_total,
         ),
     )(
-        block_of_slot, doc_lengths, queries, keys, values,
-        out_weight.reshape(dp_total, piece, width),
+        block_of_slot, doc_lengths, queries, keys, values, out_weight,
     )
 
 
@@ -371,7 +422,8 @@
             and keys.shape[1] == head_size
             and rows % 16 == 0
             and (tok_rows // 2) % rows == 0
-            and out_weight.shape[0] % (16 * dp_total) == 0
+            and out_weight.shape[0] % 128 == 0
+            and out_weight.shape[1] % (128 * dp_total) == 0
             and out_weight.shape[0] == head_size
         )
         run = functools.partial(fused, dp_total, head_total) if fits else general

time: 31.7 us -> 28.3 us (0.89)
  the two profiles are of different devices: /device:TPU:9 before, /device:TPU:0 now
where the time goes in v2:
time: 28.3 us; the launch traced here: 27.9 us
  Pallas kernels  26.1 us (92%)
  local copies, waits for them, and re-layouts  1.77 us (6%)
    pallas_call x1, Pallas kernels, fused(): pl.pallas_call(functools.partial(fused_kernel, dp_total, head_total, shar...  26.1 us
    unnamed x1, local copies, waits for them, and re-layouts  1.77 us

profile of v2, /device:TPU:0, one launch (start us, length us, event | category | flops | bytes accessed | tf_op | source)
XLA Modules:
  0.0 27.9 jit_solution(8685891532625075027)
XLA Ops:
  0.0 26.1 %shard_map.64 = bf16[96,2048]{1,0:T(8,128)(2,1)} custom-call(s32[16]{0:T(128)} %table.1, s32[4]{0:T(128)} %lengths.1, bf16[384,128]{1,0:T(8,128)(2,1)} %q_in.1, bf16[384,128]{1,0:T(8,128)(2,1)} %k_in.1, bf16[384,128]{1,0:T(8,128)(2,1)} %v_in.1, bf16[128,2048]{1,0:T(8,128)(2,1)} %w_in.1), custom_call_target="tpu_custom_call" | custom-call | flops 805306368 | bytes 1212416 | tf_op jit(solution)/shard_map/pallas_call | solution.py:375
  26.1 1.8 %copy.8 = bf16[96,2048]{1,0:T(8,128)(2,1)} copy(bf16[96,2048]{1,0:T(8,128)(2,1)} %shard_map.64) | data formatting | bytes 786432

commit v3 on v2

--- a/solution.py
+++ b/solution.py
@@ -152,6 +152,8 @@
     ]
     for copy in locals_:
         copy.start()
+    for copy in locals_:
+        copy.wait()
     pl.semaphore_wait(barrier, 3 + head_total - 1)
 
     sent = []
@@ -220,24 +222,24 @@
         arrived(part, s_recv.at[0, foreign])
         send(part, part, s_send.at[1, foreign], s_recv.at[1, foreign], (near[CORE], head))
 
-    k_pass(0, ALONG_X, k_in)
-    v_pass(0, ALONG_Y, v_in)
+    k_pass(0, ALONG_X)
+    v_pass(0, ALONG_Y)
     for mask in range(1, head_total):
         send(
-            w_in.at[pl.ds(0, shared), columns_of(0)], w_part(mask, 0, None),
+            w_part(0, 0, None), w_part(mask, 0, None),
             z_send.at[mask], z_recv.at[mask], (me, heads[mask]),
         )
-    v_pass(0, ALONG_X, v_in)
-    k_pass(0, ALONG_Y, k_in)
-    k_pass(0, CORE, k_in)
-    v_pass(0, CORE, v_in)
+    v_pass(0, ALONG_X)
+    k_pass(0, ALONG_Y)
+    k_pass(0, CORE)
+    v_pass(0, CORE)
     for mask in range(1, head_total):
         send(own_rows(heads[mask]), q_buf.at[mask], q_send.at[mask], q_recv.at[mask], (me, heads[mask]))
     if shared < depth:
         span = straight(lax.rem(me, 2))
         for mask in range(1, head_total):
             send(
-                w_in.at[span], w_buf.at[mask, span],
+                w_buf.at[0, span], w_buf.at[mask, span],
                 s_send.at[0, mask], s_recv.at[0, mask], (me, heads[mask]),
             )
 
@@ -313,8 +315,6 @@
     k_pass(DIAG, CORE)
     v_wait(DIAG)
     v_pass(DIAG, CORE)
-    for copy in locals_:
-        copy.wait()
     for mask in foreign_heads:
         arrived(q_buf.at[mask], q_recv.at[mask])
     slots = [0, ALONG_X, ALONG_Y, CORE, CORE + ALONG_X, CORE + ALONG_Y, DIAG, CORE + DIAG]

time: 28.3 us -> 27.9 us (0.986)
  no operation moved by 1% of the time
where the time goes in v3:
time: 27.9 us; the launch traced here: 27.6 us
  Pallas kernels  25.9 us (93%)
  local copies, waits for them, and re-layouts  1.77 us (6%)
    pallas_call x1, Pallas kernels, fused(): pl.pallas_call(functools.partial(fused_kernel, dp_total, head_total, shar...  25.9 us
    unnamed x1, local copies, waits for them, and re-layouts  1.77 us

profile of v3, /device:TPU:0, one launch (start us, length us, event | category | flops | bytes accessed | tf_op | source)
XLA Modules:
  0.0 27.6 jit_solution(13300378005649516130)
XLA Ops:
  0.0 25.9 %shard_map.64 = bf16[96,2048]{1,0:T(8,128)(2,1)} custom-call(s32[16]{0:T(128)} %table.1, s32[4]{0:T(128)} %lengths.1, bf16[384,128]{1,0:T(8,128)(2,1)} %q_in.1, bf16[384,128]{1,0:T(8,128)(2,1)} %k_in.1, bf16[384,128]{1,0:T(8,128)(2,1)} %v_in.1, bf16[128,2048]{1,0:T(8,128)(2,1)} %w_in.1), custom_call_target="tpu_custom_call" | custom-call | flops 805306368 | bytes 1212416 | tf_op jit(solution)/shard_map/pallas_call | solution.py:375
  25.9 1.8 %copy.8 = bf16[96,2048]{1,0:T(8,128)(2,1)} copy(bf16[96,2048]{1,0:T(8,128)(2,1)} %shard_map.64) | data formatting | bytes 786432
